TPU v7x, 32 devices: a whole 2x2x4 slice. The times are simulated.
32 devices in a mesh: groups: 2 (over x), pool: 16 (over z, y, core).
Axes of the slice: x: 2, y: 2, z: 4, core: 2. Of those that a mesh axis runs over, the one named last changes fastest.
Arguments:
- query_rows: bfloat16 [4096, 8192], P(('groups', 'pool')), parts along dimension 0, may hold values from -125 to 125
- suffix_kv: bfloat16 [4096, 2048], P(('groups', 'pool')), parts along dimension 0, may hold values from -7 to 7
- delta_codes: int32 [256, 16, 2048], P(('groups', 'pool')), parts along dimension 0, may hold values from -127 to 127
- anchors: bfloat16 [256, 2048], P(('groups', 'pool')), parts along dimension 0, may hold values from -6 to 6
- scales: float32 [256, 16], P(('groups', 'pool')), parts along dimension 0, may hold values from 0.001 to 0.01
- anchor_pos: int32 [256], P(('groups', 'pool')), parts along dimension 0, may hold values from 0 to 15
- hit_slot: int32 [64, 1], P('groups'), parts along dimension 0, may hold values from 0 to 7
- hit_owner: int32 [64, 1], P('groups'), parts along dimension 0, may hold values from 0 to 15; in each aligned block of 32 rows (0 to 31, 32 to 63, ...) at most 6 rows name the same one
Outputs:
- context: bfloat16 [4096, 8192], P(('groups', 'pool')), parts along dimension 0
There are 2 independent parts, one for each index of `groups`. A program takes and returns all parts, laid end to end along the dimension named above; each array names one. Nothing has to cross between parts.
Inputs may be any that keep to these rules, and one draw needn't show every extreme that they name: `hit_owner`: each pool device stores at most 6 of the 32 prefix pages, and some device stores exactly 6.
All inputs are finite; a program needn't handle non-finite values.
Results may differ from a plain program's by a relative error of at most 0.0045.
Values may be sent and summed in bfloat16 or wider, within the bound.
A program may use at most 448 MiB of HBM per device.

v0:
```python
import jax
import jax.numpy as jnp
import numpy as np
from jax import lax
from jax.sharding import PartitionSpec as P

H = 64
KVH = 8
MOST = 6


far_position = 1 << 30
low_score = -1e30


def expand_pages(page_codes, page_anchor, page_scale, page_anchor_pos):
    page_len = page_codes.shape[1]
    head_dim = page_codes.shape[2] // page_scale.shape[1]
    triangle = (jnp.arange(page_len)[None, :] <= jnp.arange(page_len)[:, None]).astype(jnp.float32)
    anchor_row = jnp.take(triangle, page_anchor_pos, axis=0)
    mixing = triangle[None, :, :] - anchor_row[:, None, :]
    summed = jnp.einsum(
        "pts,psc->ptc", mixing, page_codes.astype(jnp.float32), precision=lax.Precision.HIGHEST
    )
    widened = jnp.repeat(page_scale, head_dim, axis=1)
    return (page_anchor.astype(jnp.float32)[:, None, :] + widened[:, None, :] * summed).astype(
        jnp.bfloat16
    )


def local_pages(delta_codes, anchors, scales, anchor_pos, hit_slot, hit_owner, my_index):
    owners = hit_owner[:, 0]
    slot_ids = hit_slot[:, 0]
    mine = (owners == my_index).astype(jnp.int32)
    page_rank = jnp.cumsum(mine) - 1
    buffer_ids = jnp.arange(MOST, dtype=jnp.int32)
    chosen = ((mine[None, :] == 1) & (page_rank[None, :] == buffer_ids[:, None])).astype(jnp.int32)
    picked = jnp.sum(chosen * slot_ids[None, :], axis=1)
    filled = jnp.sum(chosen, axis=1) > 0
    pages_now = expand_pages(
        jnp.take(delta_codes, picked, axis=0),
        jnp.take(anchors, picked, axis=0),
        jnp.take(scales, picked, axis=0),
        jnp.take(anchor_pos, picked, axis=0),
    )
    return (pages_now, filled)


def body(query_rows, suffix_kv, delta_codes, anchors, scales, anchor_pos, hit_slot, hit_owner):
    my_index = lax.axis_index("pool")
    pool_count = lax.axis_size("pool")
    tok_rows, model_cols = query_rows.shape
    head_dim = model_cols // H
    page_len = delta_codes.shape[1]
    pages_now, filled = local_pages(
        delta_codes, anchors, scales, anchor_pos, hit_slot, hit_owner, my_index
    )
    page_rows = pages_now.reshape(MOST * page_len, suffix_kv.shape[1])
    prefix_pos = jnp.repeat(jnp.where(filled, -1, far_position), page_len).astype(jnp.int32)
    suffix_pos = my_index * tok_rows + jnp.arange(tok_rows, dtype=jnp.int32)
    score_scale = head_dim ** (-0.5)
    group_heads = H // pool_count
    share = H // KVH
    table = np.arange(pool_count) * group_heads // share
    head_view = query_rows.reshape(tok_rows, H, head_dim)
    spread_queries = lax.all_to_all(head_view, "pool", split_axis=1, concat_axis=0, tiled=True)
    key_rows = jnp.concatenate([page_rows, suffix_kv], axis=0)
    row_count = key_rows.shape[0]
    key_rows = key_rows.reshape(row_count, 2, KVH, head_dim)[:, :, table, :]
    key_pos = jnp.concatenate([prefix_pos, suffix_pos])
    pos_copies = jnp.broadcast_to(key_pos[:, None, None], (row_count, 1, pool_count))
    got_keys, got_pos = (
        lax.all_to_all(key_rows, "pool", split_axis=2, concat_axis=0, tiled=True),
        lax.all_to_all(pos_copies, "pool", split_axis=2, concat_axis=0, tiled=True),
    )
    prefix_len = MOST * page_len
    keys_split = got_keys[:, 0, 0, :].reshape(pool_count, row_count, head_dim)
    values_split = got_keys[:, 1, 0, :].reshape(pool_count, row_count, head_dim)
    pos_split = got_pos[:, 0, 0].reshape(pool_count, row_count)
    early_keys = keys_split[:, :prefix_len].reshape(pool_count * prefix_len, head_dim)
    early_values = values_split[:, :prefix_len].reshape(pool_count * prefix_len, head_dim)
    early_pos = pos_split[:, :prefix_len].reshape(pool_count * prefix_len)
    later_keys = keys_split[:, prefix_len:].reshape(pool_count * tok_rows, head_dim)
    later_values = values_split[:, prefix_len:].reshape(pool_count * tok_rows, head_dim)
    later_pos = pos_split[:, prefix_len:].reshape(pool_count * tok_rows)
    all_rows = spread_queries.shape[0]
    count = min(8, max(1, all_rows // 512))
    block = all_rows // count
    pieces = []
    for number in range(count):
        end_row = (number + 1) * block
        block_queries = spread_queries[number * block : end_row]
        block_keys = jnp.concatenate([early_keys, later_keys[:end_row]], axis=0)
        block_values = jnp.concatenate([early_values, later_values[:end_row]], axis=0)
        block_pos = jnp.concatenate([early_pos, later_pos[:end_row]])
        query_pos = number * block + jnp.arange(block, dtype=jnp.int32)
        visible = block_pos[None, :] <= query_pos[:, None]
        scores = (
            jnp.einsum("tgd,sd->gts", block_queries, block_keys, preferred_element_type=jnp.float32)
            * score_scale
        )
        scores = jnp.where(visible[None], scores, jnp.float32(low_score))
        peak = jnp.max(scores, axis=-1, keepdims=True)
        weights = jnp.where(visible[None], jnp.exp(scores - peak), jnp.float32(0.0))
        denom = jnp.sum(weights, axis=-1)
        mixed = jnp.einsum(
            "gts,sd->tgd",
            weights.astype(jnp.bfloat16),
            block_values,
            preferred_element_type=jnp.float32,
        )
        pieces.append((mixed / jnp.transpose(denom, (1, 0))[:, :, None]).astype(jnp.bfloat16))
    outputs = jnp.concatenate(pieces, axis=0)
    returned = lax.all_to_all(outputs, "pool", split_axis=0, concat_axis=1, tiled=True)
    return returned.reshape(tok_rows, model_cols)


def solution(mesh):
    placed = (
        P(("groups", "pool"), None),
        P(("groups", "pool"), None),
        P(("groups", "pool"), None, None),
        P(("groups", "pool"), None),
        P(("groups", "pool"), None),
        P(("groups", "pool")),
        P("groups", None),
        P("groups", None),
    )
    return jax.shard_map(
        body, mesh=mesh, in_specs=placed, out_specs=P(("groups", "pool"), None), check_vma=False
    )
```

profile of v0, /device:TPU:1, one launch (start us, length us, event | category | flops | bytes accessed | tf_op | source)
XLA Modules:
  0.0 271.3 jit_solution(4201610431108053348)
XLA Ops:
  2.7 7.3 %all-to-all-start.1 = ((s32[224,1,16]{0,1,2:T(1,128)}), s32[224,1,16]{0,1,2:T(1,128)S(1)}, u32[]{:S(2)}, u32[]{:S(2)}) async-start(s32[224,1,16]{0,1,2:T(1,128)} %broadcast_in_dim.179), calls=%async_computation.1 | async-start | bytes 32768 | tf_op jit(solution)/shard_map/all_to_all | solution.py:74
  10.1 1.3 gather_fusion.2
  11.4 1.2 gather_fusion.1
  12.7 1.4 gather_fusion
  14.8 1.3 copy.88
  18.2 2.0 gather_fusion.5
  20.3 6.0 %all-to-all-start = ((bf16[224,2,16,128]{3,0,1,2:T(8,128)(2,1)}), bf16[224,2,16,128]{3,0,1,2:T(8,128)(2,1)S(1)}, u32[]{:S(2)}, u32[]{:S(2)}) async-start(bf16[224,2,16,128]{3,0,1,2:T(8,128)(2,1)} %bitcast.228), calls=%async_computation | async-start | bytes 3670016 | tf_op jit(solution)/shard_map/all_to_all | solution.py:73
  26.3 4.1 %copy.94 = bf16[128,8192]{0,1:T(8,128)(2,1)} copy(bf16[128,8192]{1,0:T(8,128)(2,1)} %param.10) | data formatting | bytes 4194304 | tf_op args[0]
  30.8 32.4 %all-to-all-done = bf16[224,2,16,128]{3,0,1,2:T(8,128)(2,1)S(1)} async-done(((bf16[224,2,16,128]{3,0,1,2:T(8,128)(2,1)}), bf16[224,2,16,128]{3,0,1,2:T(8,128)(2,1)S(1)}, u32[]{:S(2)}, u32[]{:S(2)}) %all-to-all-start) | async-done | bytes 1835040 | tf_op jit(solution)/shard_map/all_to_all | solution.py:73
  63.2 1.3 copy-done.2
  64.5 10.4 %all-to-all-start.2 = ((bf16[128,64,128]{0,2,1:T(8,128)(2,1)}), bf16[128,64,128]{0,2,1:T(8,128)(2,1)S(1)}, u32[]{:S(2)}, u32[]{:S(2)}) async-start(bf16[128,64,128]{0,2,1:T(8,128)(2,1)} %bitcast.23), calls=%async_computation.2 | async-start | bytes 4194304 | tf_op jit(solution)/shard_map/all_to_all | solution.py:66
  74.9 1.6 iota_compare_fusion
  76.5 2.0 broadcast_compare_fusion.2
  78.5 2.3 broadcast_compare_fusion.1
  80.8 2.5 broadcast_compare_fusion
  90.5 1.8 copy.117
  92.3 1.9 copy.103
  94.3 2.1 copy.118
  97.3 18.9 %all-to-all-done.2 = bf16[128,64,128]{0,2,1:T(8,128)(2,1)S(1)} async-done(((bf16[128,64,128]{0,2,1:T(8,128)(2,1)}), bf16[128,64,128]{0,2,1:T(8,128)(2,1)S(1)}, u32[]{:S(2)}, u32[]{:S(2)}) %all-to-all-start.2) | async-done | bytes 2097184 | tf_op jit(solution)/shard_map/all_to_all | solution.py:66
  116.2 2.9 %copy.95 = bf16[128,64,128]{2,0,1:T(8,128)(2,1)} copy(bf16[128,64,128]{0,2,1:T(8,128)(2,1)S(1)} %all-to-all-done.2) | data formatting | bytes 4194304 | tf_op jit(solution)/shard_map/all_to_all | solution.py:66
  119.1 1.7 fusion.126
  121.8 11.6 %fusion.131 = (f32[4,512]{1,0:T(4,128)S(1)}, bf16[4,512,2048]{1,2,0:T(8,128)(2,1)}) fusion(pred[512,2048]{0,1:T(8,128)(4,1)} %iota_compare_fusion, bf16[512,4,128]{2,0,1:T(8,128)(2,1)S(1)} %bitcast.239, bf16[512,128]{1,0:T(8,128)(2,1)S(1)} %bitcast.254, bf16[1536,128]{1,0:T(8,128)(2,1)} %bitcast.242), kind=kOutput, calls=%fused_computation.161 | convolution fusion | flops 1099958272 | bytes 10493952 | tf_op jit(solution)/shard_map/sub | solution.py:104
  133.5 13.7 %fusion.130 = (f32[4,512]{1,0:T(4,128)S(1)}, bf16[4,512,2560]{1,2,0:T(8,128)(2,1)}) fusion(pred[512,2560]{0,1:T(8,128)(4,1)S(1)} %copy-done.6, bf16[512,4,128]{2,0,1:T(8,128)(2,1)S(1)} %bitcast.240, bf16[1024,128]{1,0:T(8,128)(2,1)} %bitcast.248, bf16[1536,128]{1,0:T(8,128)(2,1)S(1)} %bitcast.244), kind=kOutput, calls=%fused_computation.160 | convolution fusion | flops 1374947840 | bytes 12984320 | tf_op jit(solution)/shard_map/sub | solution.py:104
  147.2 5.6 %fusion.71 = bf16[512,4,128]{0,2,1:T(8,128)(2,1)} fusion(bf16[4,512,2048]{1,2,0:T(8,128)(2,1)} %get-tuple-element.24, bf16[512,128]{0,1:T(8,128)(2,1)S(1)} %copy-done.19, bf16[1536,128]{0,1:T(8,128)(2,1)S(1)} %copy-done.15, f32[512,4]{0,1:T(4,128)S(1)} %bitcast.256), kind=kOutput, calls=%fused_computation.65 | convolution fusion | flops 1075314688 | bytes 9445376 | tf_op jit(solution)/shard_map/gts,sd->tgd/dot_general | solution.py:106
  154.0 2.3 fusion.62
  156.3 16.0 %fusion.129 = (f32[4,512]{1,0:T(4,128)S(1)}, bf16[4,512,3072]{1,2,0:T(8,128)(2,1)}) fusion(pred[512,3072]{0,1:T(8,128)(4,1)S(1)} %copy-done.5, bf16[512,4,128]{2,0,1:T(8,128)(2,1)S(1)} %bitcast.238, bf16[1536,128]{1,0:T(8,128)(2,1)} %bitcast.246, bf16[1536,128]{1,0:T(8,128)(2,1)S(1)} %bitcast.245), kind=kOutput, calls=%fused_computation.159 | convolution fusion | flops 1649937408 | bytes 15474688 | tf_op jit(solution)/shard_map/sub | solution.py:104
  172.3 7.6 %fusion.65 = bf16[512,4,128]{0,2,1:T(8,128)(2,1)} fusion(bf16[4,512,3072]{1,2,0:T(8,128)(2,1)} %get-tuple-element.20, bf16[1536,128]{0,1:T(8,128)(2,1)} %copy.103, bf16[1536,128]{0,1:T(8,128)(2,1)} %copy.93, f32[512,4]{0,1:T(4,128)S(1)} %bitcast.259), kind=kOutput, calls=%fused_computation.63 | convolution fusion | flops 1612709888 | bytes 13901824 | tf_op jit(solution)/shard_map/gts,sd->tgd/dot_general | solution.py:106
  179.9 18.2 %fusion.128 = (f32[4,512]{1,0:T(4,128)S(1)}, bf16[4,512,3584]{1,2,0:T(8,128)(2,1)}) fusion(pred[512,3584]{0,1:T(8,128)(4,1)S(1)} %copy-done.4, bf16[512,4,128]{2,0,1:T(8,128)(2,1)S(1)} %bitcast.237, bf16[2048,128]{1,0:T(8,128)(2,1)S(1)} %bitcast.236, bf16[1536,128]{1,0:T(8,128)(2,1)} %bitcast.243), kind=kOutput, calls=%fused_computation.158 | convolution fusion | flops 1924926976 | bytes 17965056 | tf_op jit(solution)/shard_map/sub | solution.py:104
  198.1 7.5 %fusion.68 = bf16[512,4,128]{0,2,1:T(8,128)(2,1)S(1)} fusion(bf16[4,512,3584]{1,2,0:T(8,128)(2,1)} %get-tuple-element.18, bf16[2048,128]{0,1:T(8,128)(2,1)S(1)} %copy-done.8, bf16[1536,128]{0,1:T(8,128)(2,1)} %copy.93, f32[512,4]{0,1:T(4,128)S(1)} %bitcast.258), kind=kOutput, calls=%fused_computation.64 | convolution fusion | flops 1881407488 | bytes 16130048 | tf_op jit(solution)/shard_map/gts,sd->tgd/dot_general | solution.py:106
  205.9 2.5 copy.110
  208.5 58.5 %all_to_all.63 = bf16[2048,4,128]{2,1,0:T(4,128)(2,1)S(1)} all-to-all(bf16[2048,4,128]{2,1,0:T(4,128)(2,1)} %copy.110), channel_id=1, replica_groups=mesh['groups'=2,'pool'=16] {'pool'}, dimensions={0} | all-to-all | bytes 4194304 | tf_op jit(solution)/shard_map/all_to_all | solution.py:114
  268.2 2.8 %reshape.311 = bf16[128,8192]{1,0:T(8,128)(2,1)} reshape(bf16[128,16,4,128]{3,2,1,0:T(4,128)(2,1)S(1)} %copy.111) | data formatting | bytes 4194304 | tf_op jit(solution)/shard_map/reshape | solution.py:115
  (107 shorter events, 17.8 us)
Async XLA Ops:
  0.0 16.5 %copy-start = (s32[8,16,2048]{2,1,0:T(8,128)S(1)}, s32[8,16,2048]{2,1,0:T(8,128)}, u32[]{:S(2)}) copy-start(s32[8,16,2048]{2,1,0:T(8,128)} %param.12) | copy-start | bytes 3145732
  0.0 18.2 %copy-start.20 = (s32[16]{0:T(128)S(1)}, s32[16]{0:T(128)}, u32[]{:S(2)}) copy-start(s32[16]{0:T(128)} %constant.117) | copy-start | bytes 196
  2.7 17.6 %all-to-all-start.1 = ((s32[224,1,16]{0,1,2:T(1,128)}), s32[224,1,16]{0,1,2:T(1,128)S(1)}, u32[]{:S(2)}, u32[]{:S(2)}) async-start(s32[224,1,16]{0,1,2:T(1,128)} %broadcast_in_dim.179), calls=%async_computation.1 | async-start | bytes 32768 | tf_op jit(solution)/shard_map/all_to_all | solution.py:74
  20.3 42.9 %all-to-all-start = ((bf16[224,2,16,128]{3,0,1,2:T(8,128)(2,1)}), bf16[224,2,16,128]{3,0,1,2:T(8,128)(2,1)S(1)}, u32[]{:S(2)}, u32[]{:S(2)}) async-start(bf16[224,2,16,128]{3,0,1,2:T(8,128)(2,1)} %bitcast.228), calls=%async_computation | async-start | bytes 3670016 | tf_op jit(solution)/shard_map/all_to_all | solution.py:73
  63.2 1.3 copy-start.2
  64.5 51.8 %all-to-all-start.2 = ((bf16[128,64,128]{0,2,1:T(8,128)(2,1)}), bf16[128,64,128]{0,2,1:T(8,128)(2,1)S(1)}, u32[]{:S(2)}, u32[]{:S(2)}) async-start(bf16[128,64,128]{0,2,1:T(8,128)(2,1)} %bitcast.23), calls=%async_computation.2 | async-start | bytes 4194304 | tf_op jit(solution)/shard_map/all_to_all | solution.py:66
  74.9 8.4 %copy-start.3 = (bf16[224,2,16,128]{3,0,1,2:T(8,128)(2,1)S(1)}, bf16[224,2,16,128]{3,0,1,2:T(8,128)(2,1)}, u32[]{:S(2)}) copy-start(bf16[224,2,16,128]{3,0,1,2:T(8,128)(2,1)} %copy-done.2) | copy-start | bytes 5505028
  97.3 24.5 %copy-start.18 = (bf16[4,128,128]{2,1,0:T(8,128)(2,1)S(1)}, bf16[4,128,128]{2,1,0:T(8,128)(2,1)}, u32[]{:S(2)}) copy-start(bf16[4,128,128]{2,1,0:T(8,128)(2,1)} %slice.164) | copy-start | bytes 393220
  121.8 11.6 %copy-start.6 = (pred[512,2560]{0,1:T(8,128)(4,1)S(1)}, pred[512,2560]{0,1:T(8,128)(4,1)}, u32[]{:S(2)}) copy-start(pred[512,2560]{0,1:T(8,128)(4,1)} %broadcast_compare_fusion.2) | copy-start | bytes 3932164
  121.8 11.6 %copy-start.13 = (bf16[16,96,128]{2,1,0:T(8,128)(2,1)S(1)}, bf16[16,96,128]{2,1,0:T(8,128)(2,1)}, u32[]{:S(2)}) copy-start(bf16[16,96,128]{2,1,0:T(8,128)(2,1)} %slice.163) | copy-start | bytes 1179652
  133.5 13.7 %copy-start.15 = (bf16[1536,128]{0,1:T(8,128)(2,1)S(1)}, bf16[1536,128]{0,1:T(8,128)(2,1)}, u32[]{:S(2)}) copy-start(bf16[1536,128]{0,1:T(8,128)(2,1)} %copy.93) | copy-start | bytes 1179652
  133.5 13.7 %copy-start.19 = (bf16[512,128]{0,1:T(8,128)(2,1)S(1)}, bf16[512,128]{0,1:T(8,128)(2,1)}, u32[]{:S(2)}) copy-start(bf16[512,128]{0,1:T(8,128)(2,1)} %copy.116) | copy-start | bytes 393220
  147.2 5.6 %copy-start.16 = (bf16[1536,128]{0,1:T(8,128)(2,1)S(1)}, bf16[1536,128]{0,1:T(8,128)(2,1)}, u32[]{:S(2)}) copy-start(bf16[1536,128]{0,1:T(8,128)(2,1)} %copy.93) | copy-start | bytes 1179652
  147.2 5.6 %copy-start.17 = (bf16[1024,128]{0,1:T(8,128)(2,1)S(1)}, bf16[1024,128]{0,1:T(8,128)(2,1)}, u32[]{:S(2)}) copy-start(bf16[1024,128]{0,1:T(8,128)(2,1)} %copy.117) | copy-start | bytes 786436
  147.2 6.8 %copy-start.21 = (bf16[4,512,2560]{1,2,0:T(8,128)(2,1)S(1)}, bf16[4,512,2560]{1,2,0:T(8,128)(2,1)}, u32[]{:S(2)}) copy-start(bf16[4,512,2560]{1,2,0:T(8,128)(2,1)} %get-tuple-element.22) | copy-start | bytes 31457284
  154.0 2.4 copy-start.5
  154.0 2.4 copy-start.9
  154.0 2.4 copy-start.14
  172.3 7.6 %copy-start.4 = (pred[512,3584]{0,1:T(8,128)(4,1)S(1)}, pred[512,3584]{0,1:T(8,128)(4,1)}, u32[]{:S(2)}) copy-start(pred[512,3584]{0,1:T(8,128)(4,1)} %broadcast_compare_fusion) | copy-start | bytes 5505028
  172.3 7.6 %copy-start.7 = (bf16[16,128,128]{2,1,0:T(8,128)(2,1)S(1)}, bf16[16,128,128]{2,1,0:T(8,128)(2,1)}, u32[]{:S(2)}) copy-start(bf16[16,128,128]{2,1,0:T(8,128)(2,1)} %slice.176) | copy-start | bytes 1572868
  179.9 18.2 %copy-start.8 = (bf16[2048,128]{0,1:T(8,128)(2,1)S(1)}, bf16[2048,128]{0,1:T(8,128)(2,1)}, u32[]{:S(2)}) copy-start(bf16[2048,128]{0,1:T(8,128)(2,1)} %copy.118) | copy-start | bytes 1572868
  198.1 7.5 %copy-start.10 = (bf16[512,4,128]{0,2,1:T(8,128)(2,1)S(1)}, bf16[512,4,128]{0,2,1:T(8,128)(2,1)}, u32[]{:S(2)}) copy-start(bf16[512,4,128]{0,2,1:T(8,128)(2,1)} %fusion.71) | copy-start | bytes 1572868
  198.1 7.5 %copy-start.11 = (bf16[512,4,128]{0,2,1:T(8,128)(2,1)S(1)}, bf16[512,4,128]{0,2,1:T(8,128)(2,1)}, u32[]{:S(2)}) copy-start(bf16[512,4,128]{0,2,1:T(8,128)(2,1)} %fusion.62) | copy-start | bytes 1572868
  198.1 7.5 %copy-start.12 = (bf16[512,4,128]{0,2,1:T(8,128)(2,1)S(1)}, bf16[512,4,128]{0,2,1:T(8,128)(2,1)}, u32[]{:S(2)}) copy-start(bf16[512,4,128]{0,2,1:T(8,128)(2,1)} %fusion.65) | copy-start | bytes 1572868
  205.9 65.1 %copy-start.1 = (s32[8,16,2048]{2,1,0:T(8,128)S(1)}, s32[8,16,2048]{2,1,0:T(8,128)}, u32[]{:S(2)}) copy-start(s32[8,16,2048]{2,1,0:T(8,128)} %param.12) | copy-start | bytes 3145732
where the time goes:
time: 275 us; the launch traced here: 271 us
  matrix products  83.3 us (30%)
  blocking collectives  58.5 us (21%)
  waiting for transfers between devices  51.4 us (19%)
  local copies, waits for them, and re-layouts  42.8 us (16%)
  starting transfers between devices  23.8 us (9%)
  other arithmetic  10.8 us (4%)
    sub x4, matrix products, body(): weights = jnp.where(visible[None], jnp.exp(scores - peak), jnp.float32(0.0))  59.5 us
    all_to_all x1, blocking collectives, body(): lax.all_to_all(outputs, 'pool', split_axis=0, concat_axis=1, tiled=True)  58.5 us
    all_to_all x1, waiting for transfers between devices, body(): lax.all_to_all(key_rows, 'pool', split_axis=2, concat_axis=0, tiled=True)  32.4 us
    dot_general x4, matrix products, body(): jnp.einsum('gts,sd->tgd', weights.astype(jnp.bfloat16), block_values, pre...  23 us
    all_to_all x1, waiting for transfers between devices, body(): lax.all_to_all(head_view, 'pool', split_axis=1, concat_axis=0, tiled=True)  18.9 us
    all_to_all x1, starting transfers between devices, body(): lax.all_to_all(head_view, 'pool', split_axis=1, concat_axis=0, tiled=True)  10.4 us
    le x4, other arithmetic, body(): visible = block_pos[None, :] <= query_pos[:, None]  8.36 us
    unnamed x50, local copies, waits for them, and re-layouts  8.05 us
  transfers between devices with their start and end apart: 3, of which 2 were waited for; matrix products, arithmetic and copies ran while one was open for 14% of the time, Pallas kernels for 0%

commit v1 on v0

v1 whole, which is shorter than its diff:
```python
import functools
import jax
import jax.numpy as jnp
from jax import lax
from jax.experimental import pallas as pl
from jax.experimental.pallas import tpu as pltpu
from jax.sharding import PartitionSpec as P

H = 64
KVH = 8
MOST = 6

LOG2E = 1.4426950408889634


def expand_pages(page_codes, page_anchor, page_scale, page_anchor_pos):
    page_len = page_codes.shape[1]
    head_dim = page_codes.shape[2] // page_scale.shape[1]
    triangle = (jnp.arange(page_len)[None, :] <= jnp.arange(page_len)[:, None]).astype(jnp.float32)
    anchor_row = jnp.take(triangle, page_anchor_pos, axis=0)
    mixing = triangle[None, :, :] - anchor_row[:, None, :]
    summed = jnp.einsum(
        "pts,psc->ptc", mixing, page_codes.astype(jnp.float32), precision=lax.Precision.HIGHEST
    )
    widened = jnp.repeat(page_scale, head_dim, axis=1)
    return (page_anchor.astype(jnp.float32)[:, None, :] + widened[:, None, :] * summed).astype(
        jnp.bfloat16
    )


def local_pages(delta_codes, anchors, scales, anchor_pos, hit_slot, hit_owner, my_index):
    owners = hit_owner[:, 0]
    slot_ids = hit_slot[:, 0]
    mine = (owners == my_index).astype(jnp.int32)
    page_rank = jnp.cumsum(mine) - 1
    buffer_ids = jnp.arange(MOST, dtype=jnp.int32)
    chosen = ((mine[None, :] == 1) & (page_rank[None, :] == buffer_ids[:, None])).astype(jnp.int32)
    picked = jnp.sum(chosen * slot_ids[None, :], axis=1)
    filled = jnp.sum(chosen, axis=1) > 0
    pages_now = expand_pages(
        jnp.take(delta_codes, picked, axis=0),
        jnp.take(anchors, picked, axis=0),
        jnp.take(scales, picked, axis=0),
        jnp.take(anchor_pos, picked, axis=0),
    )
    return (pages_now, filled)


def flash_body(place, pages, q_ref, kp_ref, vp_ref, ks_ref, vs_ref, o_ref, qs, kb, vb, top, tot, acc, *, share, hd, page, npage, tok, blk, rt, wide):
    my = place[0]
    R = share*tok
    c = hd**-0.5*LOG2E
    for h in range(share):
        q=q_ref[:, h*hd:(h+1)*hd]
        if wide:
            qf=q.astype(jnp.float32)*c
            hi=qf.astype(jnp.bfloat16)
            qs[h*tok:(h+1)*tok,:hd]=hi
            qs[h*tok:(h+1)*tok,hd:]=(qf-hi.astype(jnp.float32)).astype(jnp.bfloat16)
        else:
            qs[h*tok:(h+1)*tok,:]=q
    for j in range(npage):
        src=pl.ds(pl.multiple_of(pages[j]*page,page),page)
        kb[j*page:(j+1)*page,:]=kp_ref[src,:]
        vb[j*page:(j+1)*page,:]=vp_ref[src,:]
    def block(k, v, first, mask_from):
        if wide: k=jnp.concatenate([k,k],axis=1)
        n=k.shape[0]
        for r in range(0,R,rt):
            rows=slice(r,r+rt)
            s=lax.dot_general(qs[rows,:],k,(((1,),(1,)),((),())),preferred_element_type=jnp.float32)
            if not wide: s=s*c
            if mask_from is not None:
                qpos=my*tok+lax.rem(lax.broadcasted_iota(jnp.int32,(rt,n),0)+r,tok)
                kpos=mask_from+lax.broadcasted_iota(jnp.int32,(rt,n),1)
                s=jnp.where(kpos<=qpos,s,-1e30)
            peak=jnp.max(s,axis=1,keepdims=True)
            if first:
                now=jnp.broadcast_to(peak,(rt,128))
            else:
                old=top[rows,:]
                now=jnp.maximum(old,peak)
            p=[jnp.exp2(s[:,i:i+128]-now) for i in range(0,n,128)]
            part=functools.reduce(jnp.add,p)
            pv=jnp.dot(jnp.concatenate([x.astype(jnp.bfloat16) for x in p],axis=1),v,preferred_element_type=jnp.float32)
            top[rows,:]=now
            if first:
                tot[rows,:]=part; acc[rows,:]=pv
            else:
                al=jnp.exp2(old-now)
                tot[rows,:]=tot[rows,:]*al+part
                acc[rows,:]=acc[rows,:]*al+pv
    npre=npage*page
    for i in range(0,npre,blk):
        block(kb[i:i+blk,:],vb[i:i+blk,:],i==0,None)
    end=(my+1)*tok
    full=lax.div(my*tok,blk)
    def step(i,_):
        at=pl.ds(pl.multiple_of(i*blk,blk),blk)
        block(ks_ref[at,:],vs_ref[at,:],False,None)
        return 0
    lax.fori_loop(0,full,step,0)
    at=pl.ds(pl.multiple_of(full*blk,blk),blk)
    block(ks_ref[at,:],vs_ref[at,:],False,full*blk)
    for h in range(share):
        rows=slice(h*tok,(h+1)*tok)
        l=jnp.sum(tot[rows,:],axis=1,keepdims=True)
        o_ref[:,h*hd:(h+1)*hd]=(acc[rows,:]/l).astype(jnp.bfloat16)

def flash(place,pages,q,page_rows,suffix,first_head,heads,kvh,share,hd,page,npage,blk=512,rt=1024,wide=False):
    tok=q.shape[0]
    total=suffix.shape[0]
    R=share*tok
    kv_cols=page_rows.shape[1]//(2*hd)
    body=functools.partial(flash_body,share=share,hd=hd,page=page,npage=npage,tok=tok,blk=blk,rt=rt,wide=wide)
    full=lambda n: (n,hd)
    return pl.pallas_call(body,
      out_shape=jax.ShapeDtypeStruct((tok,heads*share*hd),jnp.bfloat16),
      grid_spec=pltpu.PrefetchScalarGridSpec(num_scalar_prefetch=2,grid=(heads,),
        in_specs=[pl.BlockSpec((tok,share*hd),lambda g,*_:(0,first_head+g)),
          pl.BlockSpec((page_rows.shape[0],hd),lambda g,*_:(0,g)),
          pl.BlockSpec((page_rows.shape[0],hd),lambda g,*_:(0,kv_cols+g)),
          pl.BlockSpec((total,hd),lambda g,*_:(0,g)),
          pl.BlockSpec((total,hd),lambda g,*_:(0,kv_cols+g))],
        out_specs=pl.BlockSpec((tok,share*hd),lambda g,*_:(0,g)),
        scratch_shapes=[pltpu.VMEM((R,hd*(2 if wide else 1)),jnp.bfloat16),pltpu.VMEM((npage*page,hd),jnp.bfloat16),pltpu.VMEM((npage*page,hd),jnp.bfloat16),
          pltpu.VMEM((R,128),jnp.float32),pltpu.VMEM((R,128),jnp.float32),pltpu.VMEM((R,hd),jnp.float32)]),
      compiler_params=pltpu.CompilerParams(vmem_limit_bytes=50<<20,dimension_semantics=("arbitrary",)),
    )(place,pages,q,page_rows,page_rows,suffix,suffix)


def page_places(hit_owner):
    owners = hit_owner[:, 0]
    before = jnp.tril(jnp.ones((owners.shape[0],) * 2, jnp.int32), -1)
    rank = jnp.sum(before * (owners[None, :] == owners[:, None]), axis=1)
    return (owners * MOST + rank).astype(jnp.int32)


def body(query_rows, suffix_kv, delta_codes, anchors, scales, anchor_pos, hit_slot, hit_owner):
    my_index = lax.axis_index("pool")
    head_dim = query_rows.shape[1] // H
    page_len = delta_codes.shape[1]
    pages_now, _ = local_pages(
        delta_codes, anchors, scales, anchor_pos, hit_slot, hit_owner, my_index
    )
    width = suffix_kv.shape[1]
    page_rows = pages_now.reshape(MOST * page_len, width)
    mine = jnp.concatenate([page_rows, suffix_kv], axis=0)
    everyone = lax.all_gather(mine, "pool", axis=0)
    pages_all = everyone[:, : MOST * page_len].reshape(-1, width)
    suffix_all = everyone[:, MOST * page_len :].reshape(-1, width)
    place = my_index.astype(jnp.int32).reshape(1)
    return flash(place, page_places(hit_owner), query_rows, pages_all, suffix_all, 0, KVH, KVH,
                 H // KVH, head_dim, page_len, hit_slot.shape[0])


def solution(mesh):
    placed = (
        P(("groups", "pool"), None),
        P(("groups", "pool"), None),
        P(("groups", "pool"), None, None),
        P(("groups", "pool"), None),
        P(("groups", "pool"), None),
        P(("groups", "pool")),
        P("groups", None),
        P("groups", None),
    )
    return jax.shard_map(
        body, mesh=mesh, in_specs=placed, out_specs=P(("groups", "pool"), None), check_vma=False
    )
```

time: 275 us -> 196 us (0.71)
  the two profiles are of different devices: /device:TPU:1 before, /device:TPU:25 now
where the time goes in v1:
time: 196 us
  waiting for transfers between devices  113 us (58%)
  Pallas kernels  44.1 us (22%)
  local copies, waits for them, and re-layouts  20.3 us (10%)
  between operations  13.5 us (7%)
  other arithmetic  3.76 us (2%)
    all_gather x1, waiting for transfers between devices, body(): everyone = lax.all_gather(mine, 'pool', axis=0)  113 us
    pallas_call x1, Pallas kernels, flash(): pl.pallas_call(body, out_shape=jax.ShapeDtypeStruct((tok, heads * share *...  44.1 us
    slice x1, local copies, waits for them, and re-layouts, body(): suffix_all = everyone[:, MOST * page_len:].reshape(-1, width)  8.33 us
    slice x1, local copies, waits for them, and re-layouts, body(): pages_all = everyone[:, :MOST * page_len].reshape(-1, width)  6.71 us
  transfers between devices with their start and end apart: 1, of which 1 were waited for; matrix products, arithmetic and copies ran while one was open for 0% of the time, Pallas kernels for 0%

profile of v1, /device:TPU:25, one launch (start us, length us, event | category | flops | bytes accessed | tf_op | source)
XLA Modules:
  0.0 195.8 jit_solution(6622246794328246631)
XLA Ops:
  6.5 0.0 copy-start
  6.5 0.0 copy-start.2
  6.5 0.0 all-gather.3.cloned.1.call-start
  6.5 0.8 compare_convert_fusion
  7.3 0.7 fusion.11
  8.0 0.1 copy.11
  8.1 0.1 reduce-window.8
  8.1 0.1 add_reduce_fusion
  8.2 0.8 select_reduce_fusion.1
  9.0 1.3 gather_fusion.2
  10.4 1.2 gather_fusion.1
  11.6 0.6 gather_fusion.3
  12.2 0.1 broadcast_select_fusion
  12.3 0.1 broadcast_bitcast_fusion
  12.4 1.4 gather_fusion
  13.7 0.1 select_convert_fusion
  13.8 0.0 copy-done
  13.8 0.6 gather_fusion.4
  14.4 0.0 copy-start.3
  14.4 0.9 fusion.1
  15.3 0.0 copy-done.2
  15.3 1.0 pad_maximum_fusion
  16.3 0.0 all-gather.3.cloned.1.call-update
  16.4 0.0 copy-done.3
  16.4 0.2 select_reduce_fusion
  16.6 113.3 %all-gather.3.cloned.1.call-done = bf16[3584,2048]{1,0:T(8,128)(2,1)} async-done(((bf16[224,2048]{1,0:T(8,128)(2,1)}), bf16[3584,2048]{1,0:T(8,128)(2,1)}) %all-gather.3.cloned.1.call-update) | async-done | bytes 14680080 | tf_op jit(solution)/shard_map/all_gather | solution.py:149
  129.8 8.3 %slice.19 = bf16[16,128,2048]{2,1,0:T(8,128)(2,1)} slice(bf16[16,224,2048]{2,1,0:T(8,128)(2,1)} %bitcast.32), slice={[0:16], [96:224], [0:2048]} | slice | bytes 16777216 | tf_op jit(solution)/shard_map/slice | solution.py:151
  138.1 0.0 copy-start.1
  138.1 6.7 %slice.18 = bf16[16,96,2048]{2,1,0:T(8,128)(2,1)} slice(bf16[16,224,2048]{2,1,0:T(8,128)(2,1)} %bitcast.33), slice={[0:16], [0:96], [0:2048]} | slice | bytes 12582912 | tf_op jit(solution)/shard_map/slice | solution.py:150
  144.9 0.0 copy-done.1
  144.9 44.1 %shard_map.82 = bf16[128,8192]{1,0:T(8,128)(2,1)} custom-call(s32[1]{0:T(128)} %bitcast.place, s32[32]{0:T(128)S(1)} %multiply_add_fusion.pages, bf16[128,8192]{1,0:T(8,128)(2,1)S(1)} %copy-done.1, bf16[1536,2048]{1,0:T(8,128)(2,1)} %bitcast.30, bf16[1536,2048]{1,0:T(8,128)(2,1)} %bitcast.31, bf16[2048,2048]{1,0:T(8,128)(2,1)} %bitcast.28, ...), custom_call_target="tpu_custom_call" | custom-call | tf_op jit(solution)/shard_map/pallas_call | solution.py:117
  (9 shorter events, 0.1 us)
Async XLA Ops:
  6.5 7.3 %copy-start = (s32[8,16,2048]{2,1,0:T(8,128)S(1)}, s32[8,16,2048]{2,1,0:T(8,128)}, u32[]{:S(2)}) copy-start(s32[8,16,2048]{2,1,0:T(8,128)} %param.10) | copy-start | bytes 3145732
  6.5 8.8 %copy-start.2 = (bf16[128,2048]{1,0:T(8,128)(2,1)S(1)}, bf16[128,2048]{1,0:T(8,128)(2,1)}, u32[]{:S(2)}) copy-start(bf16[128,2048]{1,0:T(8,128)(2,1)} %param.9) | copy-start | bytes 1572868
  6.5 123.3 %all-gather.3.cloned.1.call-start = ((), (), s32[]{:S(2)}) async-start(), calls=%async_computation | async-start | bytes 15597568 | tf_op jit(solution)/shard_map/all_gather | solution.py:149
  14.4 1.9 copy-start.3
  138.1 6.7 %copy-start.1 = (bf16[128,8192]{1,0:T(8,128)(2,1)S(1)}, bf16[128,8192]{1,0:T(8,128)(2,1)}, u32[]{:S(2)}) copy-start(bf16[128,8192]{1,0:T(8,128)(2,1)} %q_ref.1) | copy-start | bytes 6291460
Sparse Core Ops, SparseCore 0:
  16.5 113.2 all-gather.2

commit v2 on v1

--- a/solution.py
+++ b/solution.py
@@ -46,7 +46,126 @@
     return (pages_now, filled)
 
 
-def flash_body(place, pages, q_ref, kp_ref, vp_ref, ks_ref, vs_ref, o_ref, qs, kb, vb, top, tot, acc, *, share, hd, page, npage, tok, blk, rt, wide):
+PLANE = 4
+MESH = pl.DeviceIdType.MESH
+
+
+def gather_kernel(count, chunks, page_rows, mine, out, z_sem, y_sem, c_sem, got, own_sem):
+    me = lax.axis_index("pool")
+    levels = count // PLANE
+    z = lax.div(me, PLANE)
+    y = lax.rem(lax.div(me, 2), 2)
+    c = lax.rem(me, 2)
+    y_step = 2 - 4 * y
+    y_peer, c_peer = me + y_step, me + 1 - 2 * c
+    rows, width = mine.shape
+    part = width // chunks
+
+    def cut(k):
+        return slice(k * part, (k + 1) * part)
+
+    def send(own, owner, height, k, target, sem):
+        area = (slice(0, height), cut(k))
+        source = mine.at[area] if own else out.at[(owner,) + area]
+        return pltpu.make_async_remote_copy(
+            src_ref=source, dst_ref=out.at[(owner,) + area], send_sem=sem,
+            recv_sem=got.at[k, owner], device_id={"pool": target}, device_id_type=MESH)
+
+    def each(base, action):
+        action(0, base, rows)
+        for step in range(1, levels):
+            @pl.when(z - step >= 0)
+            def _():
+                action(step, base - PLANE * step, rows)
+
+            @pl.when(z + step < levels)
+            def _():
+                action(levels - 1 + step, base + PLANE * step, page_rows)
+
+    def z_sends(k, action):
+        for step in range(1, levels):
+            @pl.when(z + step < levels)
+            def _():
+                action(send(True, me, rows, k, me + PLANE * step, z_sem.at[k, step - 1]))
+
+            @pl.when(z - step >= 0)
+            def _():
+                action(send(True, me, page_rows, k, me - PLANE * step,
+                            z_sem.at[k, levels - 2 + step]))
+
+    barrier = pltpu.get_barrier_semaphore()
+    for peer in (y_peer, c_peer):
+        pl.semaphore_signal(barrier, inc=1, device_id={"pool": peer}, device_id_type=MESH)
+    for step in range(1, levels):
+        other = lax.rem(me + PLANE * step, count)
+        pl.semaphore_signal(barrier, inc=1, device_id={"pool": other}, device_id_type=MESH)
+    pl.semaphore_wait(barrier, levels + 1)
+
+    kept = pltpu.make_async_copy(mine, out.at[me], own_sem)
+    kept.start()
+    for k in range(chunks):
+        send(True, me, rows, k, y_peer, y_sem.at[k, 0]).start()
+        z_sends(k, lambda copy: copy.start())
+        send(True, me, rows, k, c_peer, c_sem.at[k, 0]).start()
+
+    last = 2 * levels - 1
+
+    def pass_column(k):
+        def action(slot, owner, height):
+            if slot == 0:
+                return
+            send(False, owner, height, k, y_peer, y_sem.at[k, slot]).wait_recv()
+            send(False, owner, height, k, y_peer, y_sem.at[k, slot]).start()
+            send(False, owner, height, k, c_peer, c_sem.at[k, slot]).start()
+        each(me, action)
+
+    def pass_side(k):
+        def action(slot, owner, height):
+            copy = send(False, owner, height, k, c_peer, c_sem.at[k, last + slot])
+            copy.wait_recv()
+            copy.start()
+        each(y_peer, action)
+
+    for k in range(chunks):
+        pass_column(k)
+        if k:
+            pass_side(k - 1)
+    pass_side(chunks - 1)
+
+    for k in range(chunks):
+        def landed(slot, owner, height):
+            send(False, owner, height, k, c_peer, c_sem.at[k, slot]).wait_recv()
+        each(c_peer, landed)
+        each(c_peer + y_step, landed)
+        z_sends(k, lambda copy: copy.wait_send())
+
+        def left(slot, owner, height):
+            send(slot == 0, owner, height, k, y_peer, y_sem.at[k, slot]).wait_send()
+            send(slot == 0, owner, height, k, c_peer, c_sem.at[k, slot]).wait_send()
+        each(me, left)
+
+        def left_side(slot, owner, height):
+            send(False, owner, height, k, c_peer, c_sem.at[k, last + slot]).wait_send()
+        each(y_peer, left_side)
+    kept.wait()
+
+
+def gather_all(mine, count, page_rows, chunks=4):
+    rows, width = mine.shape
+    levels = count // PLANE
+    dma = pltpu.SemaphoreType.DMA
+    return pl.pallas_call(
+        functools.partial(gather_kernel, count, chunks, page_rows),
+        out_shape=jax.ShapeDtypeStruct((count, rows, width), mine.dtype),
+        in_specs=[pl.BlockSpec(memory_space=pl.ANY)],
+        out_specs=pl.BlockSpec(memory_space=pl.ANY),
+        scratch_shapes=[dma((chunks, 2 * levels - 2)), dma((chunks, 2 * levels - 1)),
+                        dma((chunks, 4 * levels - 2)), dma((chunks, count)), dma(())],
+        compiler_params=pltpu.CompilerParams(collective_id=0, has_side_effects=True),
+    )(mine)
+
+
+def flash_body(place, pages, q_ref, k_ref, v_ref, o_ref, qs, kb, vb, top, tot, acc, *, share, hd, page, npage, tok, blk, rt, wide):
     my = place[0]
     R = share*tok
     c = hd**-0.5*LOG2E
@@ -60,9 +179,10 @@
         else:
             qs[h*tok:(h+1)*tok,:]=q
     for j in range(npage):
-        src=pl.ds(pl.multiple_of(pages[j]*page,page),page)
-        kb[j*page:(j+1)*page,:]=kp_ref[src,:]
-        vb[j*page:(j+1)*page,:]=vp_ref[src,:]
+        owner, rank = lax.div(pages[j], MOST), lax.rem(pages[j], MOST)
+        src=pl.ds(pl.multiple_of(rank*page,page),page)
+        kb[j*page:(j+1)*page,:]=k_ref[owner,src,:]
+        vb[j*page:(j+1)*page,:]=v_ref[owner,src,:]
     def block(k, v, first, mask_from):
         if wide: k=jnp.concatenate([k,k],axis=1)
         n=k.shape[0]
@@ -93,40 +213,37 @@
     npre=npage*page
     for i in range(0,npre,blk):
         block(kb[i:i+blk,:],vb[i:i+blk,:],i==0,None)
-    end=(my+1)*tok
     full=lax.div(my*tok,blk)
+    head_rows, per = MOST*page, blk//tok
+    def suffix(ref,i):
+        return ref[pl.ds(i*per,per),head_rows:,:].reshape(blk,hd)
     def step(i,_):
-        at=pl.ds(pl.multiple_of(i*blk,blk),blk)
-        block(ks_ref[at,:],vs_ref[at,:],False,None)
+        block(suffix(k_ref,i),suffix(v_ref,i),False,None)
         return 0
     lax.fori_loop(0,full,step,0)
-    at=pl.ds(pl.multiple_of(full*blk,blk),blk)
-    block(ks_ref[at,:],vs_ref[at,:],False,full*blk)
+    block(suffix(k_ref,full),suffix(v_ref,full),False,full*blk)
     for h in range(share):
         rows=slice(h*tok,(h+1)*tok)
         l=jnp.sum(tot[rows,:],axis=1,keepdims=True)
         o_ref[:,h*hd:(h+1)*hd]=(acc[rows,:]/l).astype(jnp.bfloat16)
 
-def flash(place,pages,q,page_rows,suffix,first_head,heads,kvh,share,hd,page,npage,blk=512,rt=1024,wide=False):
+def flash(place,pages,q,everyone,first_head,heads,kvh,share,hd,page,npage,blk=512,rt=1024,wide=False):
     tok=q.shape[0]
-    total=suffix.shape[0]
+    count,all_rows=everyone.shape[:2]
     R=share*tok
-    kv_cols=page_rows.shape[1]//(2*hd)
+    kv_cols=everyone.shape[2]//(2*hd)
     body=functools.partial(flash_body,share=share,hd=hd,page=page,npage=npage,tok=tok,blk=blk,rt=rt,wide=wide)
-    full=lambda n: (n,hd)
     return pl.pallas_call(body,
       out_shape=jax.ShapeDtypeStruct((tok,heads*share*hd),jnp.bfloat16),
       grid_spec=pltpu.PrefetchScalarGridSpec(num_scalar_prefetch=2,grid=(heads,),
         in_specs=[pl.BlockSpec((tok,share*hd),lambda g,*_:(0,first_head+g)),
-          pl.BlockSpec((page_rows.shape[0],hd),lambda g,*_:(0,g)),
-          pl.BlockSpec((page_rows.shape[0],hd),lambda g,*_:(0,kv_cols+g)),
-          pl.BlockSpec((total,hd),lambda g,*_:(0,g)),
-          pl.BlockSpec((total,hd),lambda g,*_:(0,kv_cols+g))],
+          pl.BlockSpec((count,all_rows,hd),lambda g,*_:(0,0,g)),
+          pl.BlockSpec((count,all_rows,hd),lambda g,*_:(0,0,kv_cols+g))],
         out_specs=pl.BlockSpec((tok,share*hd),lambda g,*_:(0,g)),
         scratch_shapes=[pltpu.VMEM((R,hd*(2 if wide else 1)),jnp.bfloat16),pltpu.VMEM((npage*page,hd),jnp.bfloat16),pltpu.VMEM((npage*page,hd),jnp.bfloat16),
           pltpu.VMEM((R,128),jnp.float32),pltpu.VMEM((R,128),jnp.float32),pltpu.VMEM((R,hd),jnp.float32)]),
       compiler_params=pltpu.CompilerParams(vmem_limit_bytes=50<<20,dimension_semantics=("arbitrary",)),
-    )(place,pages,q,page_rows,page_rows,suffix,suffix)
+    )(place,pages,q,everyone,everyone)
 
 
 def page_places(hit_owner):
@@ -146,11 +263,9 @@
     width = suffix_kv.shape[1]
     page_rows = pages_now.reshape(MOST * page_len, width)
     mine = jnp.concatenate([page_rows, suffix_kv], axis=0)
-    everyone = lax.all_gather(mine, "pool", axis=0)
-    pages_all = everyone[:, : MOST * page_len].reshape(-1, width)
-    suffix_all = everyone[:, MOST * page_len :].reshape(-1, width)
+    everyone = gather_all(mine, lax.axis_size("pool"), MOST * page_len)
     place = my_index.astype(jnp.int32).reshape(1)
-    return flash(place, page_places(hit_owner), query_rows, pages_all, suffix_all, 0, KVH, KVH,
+    return flash(place, page_places(hit_owner), query_rows, everyone, 0, KVH, KVH,
                  H // KVH, head_dim, page_len, hit_slot.shape[0])
 
 

time: 196 us -> 159 us (0.81)
  waiting for transfers between devices: 113 us -> 0 us
  Pallas kernels: 44.1 us -> 147 us
  local copies, waits for them, and re-layouts: 20.3 us -> 5.24 us
  between operations: 13.5 us -> 0.1 us
    all_gather x1 -> x0, waiting for transfers between devices: 113 us -> none  [body(): everyone = lax.all_gather(mine, 'pool', axis=0)]
    pallas_call x0 -> x1, Pallas kernels: none -> 103 us  [gather_all(): pl.pallas_call(functools.partial(gather_kernel, count, chunks, page_rows)...]
    slice x2 -> x0, local copies, waits for them, and re-layouts: 15 us -> none  [the longest x1 8.33 us: body(): suffix_all = everyone[:, MOST * page_len:].reshape(-1, width)]
  transfers between devices with their start and end apart: 1 -> 0, of which waited for: 1 -> 0; matrix products, arithmetic and copies ran while one was open for 0% -> 0% of each run, Pallas kernels for 0% -> 0%
where the time goes in v2:
time: 159 us
  Pallas kernels  147 us (92%)
  local copies, waits for them, and re-layouts  5.24 us (3%)
  other arithmetic  5.15 us (3%)
    pallas_call x1, Pallas kernels, gather_all(): pl.pallas_call(functools.partial(gather_kernel, count, chunks, page_rows)...  103 us
    pallas_call x1, Pallas kernels, flash(): pl.pallas_call(body, out_shape=jax.ShapeDtypeStruct((tok, heads * share *...  44.4 us

profile of v2, /device:TPU:25, one launch (start us, length us, event | category | flops | bytes accessed | tf_op | source)
XLA Modules:
  0.0 158.5 jit_solution(15464687222978829101)
XLA Ops:
  0.0 0.0 copy-start
  0.0 0.0 copy-start.2
  0.0 0.8 fusion.11
  0.8 0.7 compare_convert_fusion
  1.4 0.9 select_reduce_fusion
  2.4 0.7 multiply_add_fusion.pages
  3.0 0.1 copy.11
  3.1 0.1 reduce-window.8
  3.2 0.1 add_reduce_fusion
  3.3 0.8 select_reduce_fusion.1
  4.1 1.3 gather_fusion.2
  5.4 0.6 gather_fusion.3
  6.0 1.2 gather_fusion.1
  7.2 0.1 broadcast_select_fusion
  7.3 1.4 gather_fusion
  8.7 0.1 select_convert_fusion
  8.7 0.1 broadcast_bitcast_fusion
  8.8 0.0 copy-done
  8.9 0.6 gather_fusion.4
  9.5 0.9 fusion.1
  10.3 0.0 copy-done.2
  10.4 1.0 pad_maximum_fusion.mine
  11.3 0.0 copy-start.1
  11.3 102.8 %shard_map.82.k_ref.v_ref = bf16[16,224,2048]{2,1,0:T(8,128)(2,1)} custom-call(bf16[224,2048]{1,0:T(8,128)(2,1)} %pad_maximum_fusion.mine), custom_call_target="tpu_custom_call" | custom-call | tf_op jit(solution)/shard_map/pallas_call | solution.py:157
  114.1 0.0 copy-done.1
  114.1 44.4 %shard_map.83 = bf16[128,8192]{1,0:T(8,128)(2,1)} custom-call(s32[1]{0:T(128)} %bitcast.place, s32[32]{0:T(128)S(1)} %multiply_add_fusion.pages, bf16[128,8192]{1,0:T(8,128)(2,1)S(1)} %copy-done.1, bf16[16,224,2048]{2,1,0:T(8,128)(2,1)} %shard_map.82.k_ref.v_ref, bf16[16,224,2048]{2,1,0:T(8,128)(2,1)} %shard_map.82.k_ref.v_ref), custom_call_target="tpu_custom_call" | custom-call | tf_op jit(solution)/shard_map/pallas_call | solution.py:236
  (8 shorter events, 0.1 us)
Async XLA Ops:
  0.0 8.8 %copy-start = (s32[8,16,2048]{2,1,0:T(8,128)S(1)}, s32[8,16,2048]{2,1,0:T(8,128)}, u32[]{:S(2)}) copy-start(s32[8,16,2048]{2,1,0:T(8,128)} %param.10) | copy-start | bytes 3145732
  0.0 10.3 %copy-start.2 = (bf16[128,2048]{1,0:T(8,128)(2,1)S(1)}, bf16[128,2048]{1,0:T(8,128)(2,1)}, u32[]{:S(2)}) copy-start(bf16[128,2048]{1,0:T(8,128)(2,1)} %param.9) | copy-start | bytes 1572868
  11.3 102.8 %copy-start.1 = (bf16[128,8192]{1,0:T(8,128)(2,1)S(1)}, bf16[128,8192]{1,0:T(8,128)(2,1)}, u32[]{:S(2)}) copy-start(bf16[128,8192]{1,0:T(8,128)(2,1)} %q_ref.1) | copy-start | bytes 6291460

commit v3 on v2

v3 whole, which is shorter than its diff:
```python
import functools
import jax
import jax.numpy as jnp
from jax import lax
from jax.experimental import pallas as pl
from jax.experimental.pallas import tpu as pltpu
from jax.sharding import PartitionSpec as P

H = 64
KVH = 8
MOST = 6

LOG2E = 1.4426950408889634


def expand_pages(page_codes, page_anchor, page_scale, page_anchor_pos):
    page_len = page_codes.shape[1]
    head_dim = page_codes.shape[2] // page_scale.shape[1]
    triangle = (jnp.arange(page_len)[None, :] <= jnp.arange(page_len)[:, None]).astype(jnp.float32)
    anchor_row = jnp.take(triangle, page_anchor_pos, axis=0)
    mixing = triangle[None, :, :] - anchor_row[:, None, :]
    summed = jnp.einsum(
        "pts,psc->ptc", mixing, page_codes.astype(jnp.float32), precision=lax.Precision.HIGHEST
    )
    widened = jnp.repeat(page_scale, head_dim, axis=1)
    return (page_anchor.astype(jnp.float32)[:, None, :] + widened[:, None, :] * summed).astype(
        jnp.bfloat16
    )


def local_pages(delta_codes, anchors, scales, anchor_pos, hit_slot, hit_owner, my_index):
    owners = hit_owner[:, 0]
    slot_ids = hit_slot[:, 0]
    mine = (owners == my_index).astype(jnp.int32)
    page_rank = jnp.cumsum(mine) - 1
    buffer_ids = jnp.arange(MOST, dtype=jnp.int32)
    chosen = ((mine[None, :] == 1) & (page_rank[None, :] == buffer_ids[:, None])).astype(jnp.int32)
    picked = jnp.sum(chosen * slot_ids[None, :], axis=1)
    filled = jnp.sum(chosen, axis=1) > 0
    pages_now = expand_pages(
        jnp.take(delta_codes, picked, axis=0),
        jnp.take(anchors, picked, axis=0),
        jnp.take(scales, picked, axis=0),
        jnp.take(anchor_pos, picked, axis=0),
    )
    return (pages_now, filled)


PLANE = 4
MESH = pl.DeviceIdType.MESH


def attend_head(my, head, at, heads, pick_ref, q_ref, kv, o_ref, qs, kb, vb, top, tot, acc, *, share, page, blk=512):
    R, hd = qs.shape
    tok = R // share
    npre = kb.shape[0]
    c = hd**-0.5 * LOG2E
    k_cols = pl.ds(pl.multiple_of(at * hd, hd), hd)
    v_cols = pl.ds(pl.multiple_of((heads + at) * hd, hd), hd)

    def q_cols(h):
        return pl.ds(pl.multiple_of((head * share + h) * hd, hd), hd)

    for h in range(share):
        qs[h * tok : (h + 1) * tok, :] = q_ref[:, q_cols(h)]
    stored = jnp.concatenate([kv[:, 0 : MOST * page, k_cols], kv[:, 0 : MOST * page, v_cols]], axis=2)
    stored = stored.reshape(-1, 2 * hd)
    for i in range(0, npre, blk):
        hits = jnp.dot(pick_ref[i : i + blk, :], stored, preferred_element_type=jnp.float32)
        hits = hits.astype(jnp.bfloat16)
        kb[i : i + blk, :] = hits[:, :hd]
        vb[i : i + blk, :] = hits[:, hd:]

    def block(k, v, first, mask_from):
        n = k.shape[0]
        s = lax.dot_general(qs[...], k, (((1,), (1,)), ((), ())), preferred_element_type=jnp.float32) * c
        if mask_from is not None:
            qpos = my * tok + lax.rem(lax.broadcasted_iota(jnp.int32, (R, n), 0), tok)
            kpos = mask_from + lax.broadcasted_iota(jnp.int32, (R, n), 1)
            s = jnp.where(kpos <= qpos, s, -1e30)
        peak = jnp.max(s, axis=1, keepdims=True)
        if first:
            now = jnp.broadcast_to(peak, (R, 128))
        else:
            old = top[...]
            now = jnp.maximum(old, peak)
        p = [jnp.exp2(s[:, i : i + 128] - now) for i in range(0, n, 128)]
        part = functools.reduce(jnp.add, p)
        pv = jnp.dot(jnp.concatenate([x.astype(jnp.bfloat16) for x in p], axis=1), v,
                     preferred_element_type=jnp.float32)
        top[...] = now
        if first:
            tot[...] = part
            acc[...] = pv
        else:
            al = jnp.exp2(old - now)
            tot[...] = tot[...] * al + part
            acc[...] = acc[...] * al + pv

    for i in range(0, npre, blk):
        block(kb[i : i + blk, :], vb[i : i + blk, :], i == 0, None)
    full = lax.div(my * tok, blk)
    head_rows, per = MOST * page, blk // tok

    def suffix(cols, i):
        return kv[pl.ds(i * per, per), head_rows:, cols].reshape(blk, hd)

    def step(i, carry):
        block(suffix(k_cols, i), suffix(v_cols, i), False, None)
        return carry

    lax.fori_loop(0, full, step, 0)
    block(suffix(k_cols, full), suffix(v_cols, full), False, full * blk)
    for h in range(share):
        rows = slice(h * tok, (h + 1) * tok)
        l = jnp.sum(tot[rows, :], axis=1, keepdims=True)
        o_ref[:, q_cols(h)] = (acc[rows, :] / l).astype(jnp.bfloat16)


def fused_kernel(count, chunks, page_rows, share, page, pick_ref, q_ref, mine, o_ref, z_sem, y_sem, c_sem,
                 got, own_sem, qs, kb, vb, top, tot, acc, *out):
    me = lax.axis_index("pool")
    levels = count // PLANE
    z = lax.div(me, PLANE)
    y = lax.rem(lax.div(me, 2), 2)
    c = lax.rem(me, 2)
    y_step = 2 - 4 * y
    y_peer, c_peer = me + y_step, me + 1 - 2 * c
    rows = mine.shape[1]

    def send(own, owner, height, k, target, sem):
        place = out[k].at[owner, 0:height]
        source = mine.at[k, 0:height] if own else place
        return pltpu.make_async_remote_copy(
            src_ref=source, dst_ref=place, send_sem=sem,
            recv_sem=got.at[k, owner], device_id={"pool": target}, device_id_type=MESH)

    def each(base, action):
        action(0, base, rows)
        for step in range(1, levels):
            @pl.when(z - step >= 0)
            def _():
                action(step, base - PLANE * step, rows)

            @pl.when(z + step < levels)
            def _():
                action(levels - 1 + step, base + PLANE * step, page_rows)

    def z_sends(k, action):
        for step in range(1, levels):
            @pl.when(z + step < levels)
            def _():
                action(send(True, me, rows, k, me + PLANE * step, z_sem.at[k, step - 1]))

            @pl.when(z - step >= 0)
            def _():
                action(send(True, me, page_rows, k, me - PLANE * step,
                            z_sem.at[k, levels - 2 + step]))

    barrier = pltpu.get_barrier_semaphore()
    for peer in (y_peer, c_peer):
        pl.semaphore_signal(barrier, inc=1, device_id={"pool": peer}, device_id_type=MESH)
    for step in range(1, levels):
        other = lax.rem(me + PLANE * step, count)
        pl.semaphore_signal(barrier, inc=1, device_id={"pool": other}, device_id_type=MESH)
    pl.semaphore_wait(barrier, levels + 1)

    kept = [pltpu.make_async_copy(mine.at[k], out[k].at[me], own_sem.at[k]) for k in range(chunks)]
    for copy in kept:
        copy.start()
    for k in range(chunks):
        send(True, me, rows, k, y_peer, y_sem.at[k, 0]).start()
        z_sends(k, lambda copy: copy.start())
        send(True, me, rows, k, c_peer, c_sem.at[k, 0]).start()

    last = 2 * levels - 1

    def pass_column(k):
        def action(slot, owner, height):
            if slot == 0:
                return
            send(False, owner, height, k, y_peer, y_sem.at[k, slot]).wait_recv()
            send(False, owner, height, k, y_peer, y_sem.at[k, slot]).start()
            send(False, owner, height, k, c_peer, c_sem.at[k, slot]).start()
        each(me, action)

    def pass_side(k):
        def action(slot, owner, height):
            copy = send(False, owner, height, k, c_peer, c_sem.at[k, last + slot])
            copy.wait_recv()
            copy.start()
        each(y_peer, action)

    def arrive(k):
        def landed(slot, owner, height):
            send(False, owner, height, k, c_peer, c_sem.at[k, slot]).wait_recv()
        each(c_peer, landed)
        each(c_peer + y_step, landed)
        kept[k].wait()

    def attend(k):
        heads = mine.shape[2] // (2 * qs.shape[1])

        def one(at, carry):
            attend_head(me, k * heads + at, at, heads, pick_ref, q_ref, out[k], o_ref,
                        qs, kb, vb, top, tot, acc, share=share, page=page)
            return carry
        lax.fori_loop(0, heads, one, 0)

    for k in range(chunks):
        pass_column(k)
        if k:
            pass_side(k - 1)
            arrive(k - 1)
            attend(k - 1)
    pass_side(chunks - 1)
    arrive(chunks - 1)
    attend(chunks - 1)

    for k in range(chunks):
        z_sends(k, lambda copy: copy.wait_send())

        def left(slot, owner, height):
            send(slot == 0, owner, height, k, y_peer, y_sem.at[k, slot]).wait_send()
            send(slot == 0, owner, height, k, c_peer, c_sem.at[k, slot]).wait_send()
        each(me, left)

        def left_side(slot, owner, height):
            send(False, owner, height, k, c_peer, c_sem.at[k, last + slot]).wait_send()
        each(y_peer, left_side)


def gather_attend(pick, query_rows, mine, count, page, head_dim):
    chunks, rows, width = mine.shape
    levels = count // PLANE
    share = H // KVH
    tall = share * query_rows.shape[0]
    dma = pltpu.SemaphoreType.DMA
    vmem = pl.BlockSpec(memory_space=pltpu.VMEM)
    return pl.pallas_call(
        functools.partial(fused_kernel, count, chunks, MOST * page, share, page),
        out_shape=jax.ShapeDtypeStruct(query_rows.shape, jnp.bfloat16),
        in_specs=[vmem, vmem, pl.BlockSpec(memory_space=pl.ANY)],
        out_specs=vmem,
        scratch_shapes=[dma((chunks, 2 * levels - 2)), dma((chunks, 2 * levels - 1)),
                        dma((chunks, 4 * levels - 2)), dma((chunks, count)), dma((chunks,)),
                        pltpu.VMEM((tall, head_dim), jnp.bfloat16),
                        pltpu.VMEM((pick.shape[0], head_dim), jnp.bfloat16),
                        pltpu.VMEM((pick.shape[0], head_dim), jnp.bfloat16),
                        pltpu.VMEM((tall, 128), jnp.float32), pltpu.VMEM((tall, 128), jnp.float32),
                        pltpu.VMEM((tall, head_dim), jnp.float32)]
        + [pltpu.VMEM((count, rows, width), mine.dtype)] * chunks,
        compiler_params=pltpu.CompilerParams(
            collective_id=0, has_side_effects=True, vmem_limit_bytes=56 << 20),
    )(pick, query_rows, mine)


def page_places(hit_owner):
    owners = hit_owner[:, 0]
    before = jnp.tril(jnp.ones((owners.shape[0],) * 2, jnp.int32), -1)
    rank = jnp.sum(before * (owners[None, :] == owners[:, None]), axis=1)
    return (owners * MOST + rank).astype(jnp.int32)


def body(query_rows, suffix_kv, delta_codes, anchors, scales, anchor_pos, hit_slot, hit_owner):
    my_index = lax.axis_index("pool")
    head_dim = query_rows.shape[1] // H
    page_len = delta_codes.shape[1]
    pages_now, _ = local_pages(
        delta_codes, anchors, scales, anchor_pos, hit_slot, hit_owner, my_index
    )
    width = suffix_kv.shape[1]
    page_rows = pages_now.reshape(MOST * page_len, width)
    mine = jnp.concatenate([page_rows, suffix_kv], axis=0)
    chunks = 4
    mine = mine.reshape(mine.shape[0], 2, chunks, width // (2 * chunks)).transpose(2, 0, 1, 3)
    mine = mine.reshape(chunks, -1, width // chunks)
    count = lax.axis_size("pool")
    wanted = page_places(hit_owner)[:, None] * page_len + jnp.arange(page_len, dtype=jnp.int32)
    stored = jnp.arange(count * MOST * page_len, dtype=jnp.int32)
    pick = (wanted.reshape(-1, 1) == stored[None, :]).astype(jnp.bfloat16)
    return gather_attend(pick, query_rows, mine, count,
                         page_len, head_dim)


def solution(mesh):
    placed = (
        P(("groups", "pool"), None),
        P(("groups", "pool"), None),
        P(("groups", "pool"), None, None),
        P(("groups", "pool"), None),
        P(("groups", "pool"), None),
        P(("groups", "pool")),
        P("groups", None),
        P("groups", None),
    )
    return jax.shard_map(
        body, mesh=mesh, in_specs=placed, out_specs=P(("groups", "pool"), None), check_vma=False
    )
```

time: 159 us -> 148 us (0.931)
  Pallas kernels: 147 us -> 127 us
  local copies, waits for them, and re-layouts: 5.24 us -> 12.3 us
  other arithmetic: 5.15 us -> 6.86 us
    pallas_call x2 -> x1, Pallas kernels: 147 us -> 127 us  [gather_attend(): pl.pallas_call(functools.partial(fused_kernel, count, chunks, MOST * page...]
    unnamed x8 -> x5, local copies, waits for them, and re-layouts: 0.11 us -> 3.19 us
    concatenate x0 -> x4, local copies, waits for them, and re-layouts: none -> 2.42 us  [body(): mine = jnp.concatenate([page_rows, suffix_kv], axis=0)]
where the time goes in v3:
time: 148 us; the launch traced here: 147 us
  Pallas kernels  127 us (86%)
  local copies, waits for them, and re-layouts  12.3 us (8%)
  other arithmetic  6.86 us (5%)
    pallas_call x1, Pallas kernels, gather_attend(): pl.pallas_call(functools.partial(fused_kernel, count, chunks, MOST * page...  127 us
    unnamed x5, local copies, waits for them, and re-layouts  3.19 us

profile of v3, /device:TPU:25, one launch (start us, length us, event | category | flops | bytes accessed | tf_op | source)
XLA Modules:
  0.0 147.1 jit_solution(9491413378829790411)
XLA Ops:
  0.0 0.0 copy-start
  0.0 0.7 fusion.12
  0.8 0.7 compare_convert_fusion
  1.4 0.9 select_reduce_fusion
  2.3 0.7 fusion.15
  3.0 0.1 iota_add_fusion
  3.1 0.1 add.100
  3.2 0.1 copy.15
  3.2 0.1 reduce-window.8
  3.3 0.1 add_reduce_fusion
  3.4 0.8 select_reduce_fusion.1
  4.2 1.3 gather_fusion.2
  5.6 0.6 gather_fusion.3
  6.1 1.2 gather_fusion.1
  7.4 0.1 broadcast_select_fusion
  7.4 1.4 gather_fusion
  8.8 0.1 select_convert_fusion
  8.9 0.1 broadcast_bitcast_fusion
  9.0 1.4 concatenate.9
  10.4 0.4 copy.17
  10.8 0.0 copy-done
  10.8 0.6 gather_fusion.4
  11.4 0.9 fusion.2
  12.3 0.3 concatenate.8
  12.6 0.3 copy.16
  12.9 1.2 maximum_bitcast_fusion
  14.1 1.5 %reshape.149.mine = bf16[4,224,512]{2,1,0:T(8,128)(2,1)} reshape(bf16[4,224,2,256]{3,2,1,0:T(2,128)(2,1)S(1)} %maximum_bitcast_fusion) | data formatting | bytes 1835008 | tf_op jit(solution)/shard_map/reshape | solution.py:277
  15.6 1.5 fusion.pick_ref
  17.1 126.9 %shard_map.82 = bf16[128,8192]{1,0:T(8,128)(2,1)} custom-call(bf16[512,1536]{1,0:T(8,128)(2,1)} %fusion.pick_ref, bf16[128,8192]{1,0:T(8,128)(2,1)} %q_ref.1, bf16[4,224,512]{2,1,0:T(8,128)(2,1)} %reshape.149.mine), custom_call_target="tpu_custom_call" | custom-call | tf_op jit(solution)/shard_map/pallas_call | solution.py:240
  144.0 3.1 %copy.22 = bf16[128,8192]{1,0:T(8,128)(2,1)} copy(bf16[128,8192]{1,0:T(8,128)(2,1)} %shard_map.82) | data formatting | bytes 4194304
  (8 shorter events, 0.1 us)
Async XLA Ops:
  0.0 10.8 %copy-start = (s32[8,16,2048]{2,1,0:T(8,128)S(1)}, s32[8,16,2048]{2,1,0:T(8,128)}, u32[]{:S(2)}) copy-start(s32[8,16,2048]{2,1,0:T(8,128)} %param.10) | copy-start | bytes 3145732
